TPU v7x, 32 devices: a whole 2x2x4 slice. The times are simulated.
32 devices in a mesh: gx: 2 (over core), gy: 4 (over y, x), gz: 4 (over z).
Axes of the slice: x: 2, y: 2, z: 4, core: 2. Of those that a mesh axis runs over, the one named last changes fastest.
Arguments:
- dual_matrix: float32 [2, 4, 4, 1536, 1536], P('gx', 'gy', 'gz'), may hold values from -1 to 4, as said below
- modes: float32 [2, 4, 4, 6, 1536], P('gx', 'gy', 'gz'), may hold values from -0.15625 to 0.15625
- coarse_rows: float32 [192, 192], P(('gx', 'gy', 'gz')), may hold values from -0.2 to 0.4, as said below
- loads: float32 [2, 4, 4, 8, 6, 128], P('gx', 'gy', 'gz'), may hold values from -40 to 40
- face_counts: int32 [2, 4, 4, 3], replicated, may hold values from 32 to 128
- contact: int32 [2, 4, 4, 6, 128], P('gx', 'gy', 'gz'), may hold values 0 or 1
Outputs:
- multipliers: float32 [2, 4, 4, 8, 6, 128], P('gx', 'gy', 'gz')
- residual: float32 [2, 4, 4, 8, 6, 128], P('gx', 'gy', 'gz')
Inputs may be any that keep to these rules, and one draw needn't show every extreme that they name: `dual_matrix`: every subdomain's matrix is symmetric positive definite. `coarse_rows`: the coarse operator is symmetric positive definite.
All inputs are finite; a program needn't handle non-finite values. No bound on the sum of `contact` on one device may be relied on, other than what follows from the above.
Results may differ from a plain program's by a relative error of at most 0.0003.
Values sent between devices are 32-bit elements; how exact they have to be, the bound alone decides.
A program may use at most 128 MiB of HBM per device.

v0:
```python
import jax
import jax.numpy as jnp
from jax import lax
from jax.sharding import PartitionSpec as P

ITERS = 4
highest = lax.Precision.HIGHEST


def from_behind(block, axis, distance):
    devices = range(lax.axis_size(axis))
    route = [((i - distance) % len(devices), i) for i in devices]
    return lax.ppermute(block, axis, route)


def trade(upper_faces, lower_faces):
    from_below = [
        from_behind(upper_faces[0], "gx", 1),
        from_behind(upper_faces[1], "gy", 1),
        from_behind(upper_faces[2], "gz", 1),
    ]
    from_above = [
        from_behind(lower_faces[0], "gx", -1),
        from_behind(lower_faces[1], "gy", -1),
        from_behind(lower_faces[2], "gz", -1),
    ]
    return (from_below, from_above)


def spread_faces(owned_vec):
    upper_faces = [owned_vec[..., 2 * grid_axis + 1, :] for grid_axis in range(3)]
    lower_faces = [owned_vec[..., 2 * grid_axis, :] for grid_axis in range(3)]
    from_below, from_above = trade(upper_faces, lower_faces)
    faces = []
    for grid_axis in range(3):
        faces.append(jnp.concatenate([from_below[grid_axis], lower_faces[grid_axis]], axis=-1))
        faces.append(jnp.concatenate([upper_faces[grid_axis], from_above[grid_axis]], axis=-1))
    return jnp.stack(faces, axis=-2)


def collect_faces(local_form):
    half_width = local_form.shape[-1] // 2
    upper_faces = [local_form[..., 2 * grid_axis + 1, half_width:] for grid_axis in range(3)]
    lower_faces = [local_form[..., 2 * grid_axis, :half_width] for grid_axis in range(3)]
    from_below, from_above = trade(upper_faces, lower_faces)
    pieces = []
    for grid_axis in range(3):
        pieces.append(local_form[..., 2 * grid_axis, half_width:] + from_below[grid_axis])
        pieces.append(local_form[..., 2 * grid_axis + 1, :half_width] + from_above[grid_axis])
    return jnp.stack(pieces, axis=-2)


def coarse_weights(flattened, own_modes, coarse_rows):
    on_modes = jnp.einsum("jm,km->jk", own_modes, flattened, precision=highest)
    return jnp.dot(
        coarse_rows,
        lax.all_gather(on_modes, ("gx", "gy", "gz"), axis=0, tiled=True),
        precision=highest,
    )


def on_device(dual_matrix, modes, coarse_rows, loads, face_counts, contact):
    half_width = loads.shape[-1]
    case_count = loads.shape[3]
    grid_pos = [lax.axis_index("gx"), lax.axis_index("gy"), lax.axis_index("gz")]
    grid_sizes = [lax.axis_size("gx"), lax.axis_size("gy"), lax.axis_size("gz")]

    def counts_at(where):
        return lax.dynamic_slice(
            face_counts, (where[0], where[1], where[2], 0), (1, 1, 1, 3)
        ).reshape(3)

    own_counts = counts_at(grid_pos)
    positions = jnp.arange(half_width, dtype=jnp.int32)
    own_masks = []
    local_masks = []
    for grid_axis in range(3):
        lower_pos = list(grid_pos)
        lower_pos[grid_axis] = (grid_pos[grid_axis] - 1 + grid_sizes[grid_axis]) % grid_sizes[
            grid_axis
        ]
        lower_count = counts_at(lower_pos)[grid_axis]
        lower_row = (positions < lower_count).astype(jnp.float32)
        upper_row = (positions < own_counts[grid_axis]).astype(jnp.float32)
        own_masks.extend([lower_row, upper_row])
        local_masks.extend(
            [jnp.concatenate([lower_row, lower_row]), jnp.concatenate([upper_row, upper_row])]
        )
    active_own = jnp.stack(own_masks).reshape(1, 1, 1, 1, 6, half_width)
    is_contact = contact[:, :, :, None] == 1
    matrix = dual_matrix[0, 0, 0]
    own_modes = modes[0, 0, 0]

    def local_coarse(local_form):
        flattened = local_form.reshape(case_count, -1)
        weights = coarse_weights(flattened, own_modes, coarse_rows)
        return jnp.einsum("jk,jm->km", weights, own_modes, precision=highest).reshape(
            local_form.shape
        )

    def project(vector):
        return vector - collect_faces(local_coarse(spread_faces(vector))) * active_own

    start_vector = loads * active_own

    def partial_inner(first, second):
        return jnp.sum(first * second, axis=(0, 1, 2, 4, 5))

    multipliers = jnp.zeros(loads.shape, jnp.float32)
    residual = start_vector

    def energy_sum(first, second):
        return lax.psum(partial_inner(first, second), ("gx", "gy", "gz")).reshape(-1, 1, 1)

    precond = project(residual)
    direction = precond
    energy = energy_sum(residual, precond)
    for rounds in range(ITERS):
        local_local_form = spread_faces(direction)
        local_flattened = local_local_form.reshape(case_count, -1)
        dual_image = (
            collect_faces(
                jnp.dot(local_flattened, matrix, precision=highest).reshape(local_local_form.shape)
            )
            * active_own
        )
        curvature = lax.psum(partial_inner(direction, dual_image), ("gx", "gy", "gz")).reshape(
            -1, 1, 1
        )
        step_size = energy / curvature
        updated = multipliers + step_size * direction
        multipliers = jnp.where(is_contact, jnp.maximum(updated, 0.0), updated)
        residual = residual - step_size * dual_image
        if rounds + 1 < ITERS:
            precond = project(residual)
            energy_next = energy_sum(residual, precond)
            direction = precond + energy_next / energy * direction
            energy = energy_next
    return (multipliers, residual)


def solution(mesh):
    return jax.shard_map(
        on_device,
        mesh=mesh,
        in_specs=(
            P("gx", "gy", "gz", None, None),
            P("gx", "gy", "gz", None, None),
            P(("gx", "gy", "gz"), None),
            P("gx", "gy", "gz", None, None, None),
            P(),
            P("gx", "gy", "gz", None, None),
        ),
        out_specs=(P("gx", "gy", "gz", None, None, None), P("gx", "gy", "gz", None, None, None)),
        check_vma=False,
    )
```

profile of v0, /device:TPU:0, one launch (start us, length us, event | category | flops | bytes accessed | tf_op | source)
XLA Modules:
  0.0 787.7 jit_solution(9719686072488246595)
XLA Ops:
  7.4 2.9 collective-permute-start.2
  11.3 2.1 collective-permute-start.4
  14.1 2.1 collective-permute-start.5
  18.8 67.1 %all-gather = f32[32,6,8]{2,1,0:T(8,128)S(1)} all-gather(f32[1,6,8]{2,1,0:T(8,128)S(1)} %bitcast.1086), channel_id=1, replica_groups=mesh['gx'=2,'gy'=4,'gz'=4] {'gx','gy','gz'}, dimensions={0}, use_global_device_ids=true | all-gather | bytes 6336 | tf_op jit(solution)/shard_map/all_gather | solution.py:57
  86.5 2.4 collective-permute-start.6
  89.0 1.6 collective-permute-start.8
  91.9 3.9 collective-permute-start.11
  95.8 4.1 collective-permute-done.9
  100.8 9.6 %copy.36 = f32[1,1,1,1536,1536]{3,4,2,1,0:T(8,128)} copy(f32[1,1,1,1536,1536]{4,3,2,1,0:T(8,128)} %param.6) | data formatting | bytes 18874368 | tf_op args[0]
  110.9 3.8 collective-permute-start.14
  114.7 3.9 collective-permute-start.17
  120.1 10.1 %convolution_bitcast_fusion.6 = f32[1,1,1,8,6,256]{5,3,4,2,1,0:T(8,128)S(1)} fusion(f32[8,1536,1]{1,0,2:T(8,128)S(1)} %bitcast.1078, f32[6,256,1536]{2,1,0:T(8,128)} %bitcast.1070), kind=kOutput, calls=%fused_computation.6 | convolution fusion | flops 226492416 | bytes 9535488 | tf_op jit(solution)/shard_map/dot_general | solution.py:123
  130.8 2.9 collective-permute-start.20
  134.9 2.8 collective-permute-start.23
  139.4 41.9 %all-reduce = (f32[8]{0:T(128)S(1)}, f32[8]{0:T(128)S(1)}) all-reduce(f32[8]{0:T(128)S(1)} %get-tuple-element.3, f32[8]{0:T(128)S(1)} %get-tuple-element.2), channel_id=1, replica_groups=mesh['gx'=2,'gy'=4,'gz'=4] {'gx','gy','gz'}, use_global_device_ids=true, to_apply=%region_1.2 | all-reduce | flops 16 | bytes 128 | tf_op jit(solution)/shard_map/psum | solution.py:113
  181.9 2.3 collective-permute-start.26
  185.5 1.8 collective-permute-start.28
  187.4 2.0 collective-permute-start.29
  189.4 1.5 collective-permute-done.28
  191.2 67.3 %all-gather.1 = f32[32,6,8]{2,1,0:T(8,128)S(1)} all-gather(f32[1,6,8]{2,1,0:T(8,128)S(1)} %bitcast.1087), channel_id=1, replica_groups=mesh['gx'=2,'gy'=4,'gz'=4] {'gx','gy','gz'}, dimensions={0}, use_global_device_ids=true | all-gather | bytes 6336 | tf_op jit(solution)/shard_map/all_gather | solution.py:57
  259.1 2.5 collective-permute-start.30
  262.7 1.9 collective-permute-start.33
  264.6 3.8 collective-permute-start.35
  268.4 3.6 collective-permute-done.33
  272.2 42.4 %psum.58 = f32[8]{0:T(128)S(1)} all-reduce(f32[8]{0:T(128)S(1)} %multiply_reduce_fusion.5), channel_id=1, replica_groups=mesh['gx'=2,'gy'=4,'gz'=4] {'gx','gy','gz'}, use_global_device_ids=true, to_apply=%region_5.6 | all-reduce | flops 8 | bytes 64 | tf_op jit(solution)/shard_map/psum | solution.py:113
  315.2 2.3 collective-permute-start.38
  318.9 2.1 collective-permute-start.40
  321.1 1.7 collective-permute-start.41
  324.7 10.1 %convolution_bitcast_fusion.4 = f32[1,1,1,8,6,256]{5,3,4,2,1,0:T(8,128)S(1)} fusion(f32[8,1536,1]{1,0,2:T(8,128)S(1)} %bitcast.1079, f32[6,256,1536]{2,1,0:T(8,128)} %bitcast.1071), kind=kOutput, calls=%fused_computation.4 | convolution fusion | flops 226492416 | bytes 9535488 | tf_op jit(solution)/shard_map/dot_general | solution.py:123
  336.1 2.2 collective-permute-start.45
  339.7 2.4 collective-permute-start.47
  342.2 1.5 collective-permute-done.46
  343.8 39.2 %psum.59 = f32[8]{0:T(128)S(1)} all-reduce(f32[8]{0:T(128)S(1)} %multiply_reduce_fusion.4), channel_id=1, replica_groups=mesh['gx'=2,'gy'=4,'gz'=4] {'gx','gy','gz'}, use_global_device_ids=true, to_apply=%region_7.8 | all-reduce | flops 8 | bytes 64 | tf_op jit(solution)/shard_map/psum | solution.py:127
  383.7 2.3 collective-permute-start.50
  386.9 2.2 collective-permute-start.52
  389.1 1.6 collective-permute-start.53
  393.0 66.9 %all-gather.2 = f32[32,6,8]{2,1,0:T(8,128)S(1)} all-gather(f32[1,6,8]{2,1,0:T(8,128)S(1)} %bitcast.1088), channel_id=1, replica_groups=mesh['gx'=2,'gy'=4,'gz'=4] {'gx','gy','gz'}, dimensions={0}, use_global_device_ids=true | all-gather | bytes 6336 | tf_op jit(solution)/shard_map/all_gather | solution.py:57
  460.4 2.5 collective-permute-start.54
  466.0 3.8 collective-permute-start.59
  469.8 4.1 collective-permute-done.57
  474.1 42.4 %psum.60 = f32[8]{0:T(128)S(1)} all-reduce(f32[8]{0:T(128)S(1)} %multiply_reduce_fusion.3), channel_id=1, replica_groups=mesh['gx'=2,'gy'=4,'gz'=4] {'gx','gy','gz'}, use_global_device_ids=true, to_apply=%region_9.10 | all-reduce | flops 8 | bytes 64 | tf_op jit(solution)/shard_map/psum | solution.py:113
  517.1 2.3 collective-permute-start.62
  520.8 2.1 collective-permute-start.64
  523.0 1.7 collective-permute-start.65
  526.6 10.1 %convolution_bitcast_fusion.2 = f32[1,1,1,8,6,256]{5,3,4,2,1,0:T(8,128)S(1)} fusion(f32[8,1536,1]{1,0,2:T(8,128)S(1)} %bitcast.1080, f32[6,256,1536]{2,1,0:T(8,128)} %bitcast.1072), kind=kOutput, calls=%fused_computation.2 | convolution fusion | flops 226492416 | bytes 9535488 | tf_op jit(solution)/shard_map/dot_general | solution.py:123
  537.9 2.2 collective-permute-start.69
  541.6 2.4 collective-permute-start.71
  544.1 1.5 collective-permute-done.70
  545.7 39.2 %psum.61 = f32[8]{0:T(128)S(1)} all-reduce(f32[8]{0:T(128)S(1)} %multiply_reduce_fusion.2), channel_id=1, replica_groups=mesh['gx'=2,'gy'=4,'gz'=4] {'gx','gy','gz'}, use_global_device_ids=true, to_apply=%region_11.12 | all-reduce | flops 8 | bytes 64 | tf_op jit(solution)/shard_map/psum | solution.py:127
  585.6 2.3 collective-permute-start.74
  588.8 2.2 collective-permute-start.76
  591.0 1.6 collective-permute-start.77
  594.9 66.9 %all-gather.3 = f32[32,6,8]{2,1,0:T(8,128)S(1)} all-gather(f32[1,6,8]{2,1,0:T(8,128)S(1)} %bitcast.1089), channel_id=1, replica_groups=mesh['gx'=2,'gy'=4,'gz'=4] {'gx','gy','gz'}, dimensions={0}, use_global_device_ids=true | all-gather | bytes 6336 | tf_op jit(solution)/shard_map/all_gather | solution.py:57
  662.3 2.5 collective-permute-start.78
  667.9 3.8 collective-permute-start.83
  671.7 4.1 collective-permute-done.81
  676.0 42.4 %psum.62 = f32[8]{0:T(128)S(1)} all-reduce(f32[8]{0:T(128)S(1)} %multiply_reduce_fusion.1), channel_id=1, replica_groups=mesh['gx'=2,'gy'=4,'gz'=4] {'gx','gy','gz'}, use_global_device_ids=true, to_apply=%region_13.14 | all-reduce | flops 8 | bytes 64 | tf_op jit(solution)/shard_map/psum | solution.py:113
  719.0 2.3 collective-permute-start.86
  722.7 2.1 collective-permute-start.88
  724.8 1.7 collective-permute-start.89
  728.5 10.1 %convolution_bitcast_fusion = f32[1,1,1,8,6,256]{5,3,4,2,1,0:T(8,128)S(1)} fusion(f32[8,1536,1]{1,0,2:T(8,128)S(1)} %bitcast.1081, f32[6,256,1536]{2,1,0:T(8,128)} %bitcast.1073), kind=kOutput, calls=%fused_computation | convolution fusion | flops 226492416 | bytes 9535488 | tf_op jit(solution)/shard_map/dot_general | solution.py:123
  739.9 2.2 collective-permute-start.93
  743.5 2.4 collective-permute-start.95
  747.7 39.3 %psum.63 = f32[8]{0:T(128)S(1)} all-reduce(f32[8]{0:T(128)S(1)} %multiply_reduce_fusion), channel_id=1, replica_groups=mesh['gx'=2,'gy'=4,'gz'=4] {'gx','gy','gz'}, use_global_device_ids=true, to_apply=%region_15.16 | all-reduce | flops 8 | bytes 64 | tf_op jit(solution)/shard_map/psum | solution.py:127
  (316 shorter events, 60.6 us)
Async XLA Ops:
  6.9 7.2 collective-permute-start
  7.3 8.9 %collective-permute-start.1 = (f32[1,1,1,8,128]{4,3,2,1,0:T(8,128)S(1)}, f32[1,1,1,8,128]{4,3,2,1,0:T(8,128)S(1)}, u32[]{:S(2)}, u32[]{:S(2)}) collective-permute-start(f32[1,1,1,8,128]{4,3,2,1,0:T(8,128)S(1)} %get-tuple-element.100), channel_id=1, source_target_pairs={{16,0},{0,16},{17,1},{1,17},{18,2},{2,18},{19,3},{3,19},{20,4},{4,... | collective-permute-start | bytes 12296 | tf_op jit(solution)/shard_map/ppermute | solution.py:13
  7.4 8.8 %collective-permute-start.2 = (f32[1,1,1,8,128]{4,3,2,1,0:T(8,128)S(1)}, f32[1,1,1,8,128]{4,3,2,1,0:T(8,128)S(1)}, u32[]{:S(2)}, u32[]{:S(2)}) collective-permute-start(f32[1,1,1,8,128]{4,3,2,1,0:T(8,128)S(1)} %get-tuple-element.99), channel_id=1, source_target_pairs={{12,0},{0,4},{4,8},{8,12},{13,1},{1,5},{5,9},{9,13},{14,2},{2,6},{... | collective-permute-start | bytes 12296 | tf_op jit(solution)/shard_map/ppermute | solution.py:13
  10.3 5.9 collective-permute-start.3
  11.3 5.7 collective-permute-start.4
  86.5 5.4 collective-permute-start.6
  88.9 6.9 collective-permute-start.7
  89.0 6.8 collective-permute-start.8
  90.6 9.4 %collective-permute-start.9 = (f32[1,1,1,8,128]{4,3,2,1,0:T(8,128)S(1)}, f32[1,1,1,8,128]{4,3,2,1,0:T(8,128)S(1)}, u32[]{:S(2)}, u32[]{:S(2)}) collective-permute-start(f32[1,1,1,8,128]{4,3,2,1,0:T(8,128)S(1)} %get-tuple-element.50), channel_id=1, source_target_pairs={{4,0},{8,4},{12,8},{0,12},{5,1},{9,5},{13,9},{1,13},{6,2},{10,6},{... | collective-permute-start | bytes 12296 | tf_op jit(solution)/shard_map/ppermute | solution.py:13
  91.9 8.0 %collective-permute-start.10 = (f32[1,1,1,8,128]{4,3,2,1,0:T(8,128)S(1)}, f32[1,1,1,8,128]{4,3,2,1,0:T(8,128)S(1)}, u32[]{:S(2)}, u32[]{:S(2)}) collective-permute-start(f32[1,1,1,8,128]{4,3,2,1,0:T(8,128)S(1)} %get-tuple-element.49), channel_id=1, source_target_pairs={{3,0},{0,1},{1,2},{2,3},{7,4},{4,5},{5,6},{6,7},{11,8},{8,9},{9,10... | collective-permute-start | bytes 12296 | tf_op jit(solution)/shard_map/ppermute | solution.py:13
  91.9 8.0 %collective-permute-start.11 = (f32[1,1,1,8,128]{4,3,2,1,0:T(8,128)S(1)}, f32[1,1,1,8,128]{4,3,2,1,0:T(8,128)S(1)}, u32[]{:S(2)}, u32[]{:S(2)}) collective-permute-start(f32[1,1,1,8,128]{4,3,2,1,0:T(8,128)S(1)} %get-tuple-element.48), channel_id=1, source_target_pairs={{1,0},{2,1},{3,2},{0,3},{5,4},{6,5},{7,6},{4,7},{9,8},{10,9},{11,1... | collective-permute-start | bytes 12296 | tf_op jit(solution)/shard_map/ppermute | solution.py:13
  100.7 14.0 %collective-permute-start.12 = (f32[1,1,1,8,128]{4,3,2,1,0:T(8,128)S(1)}, f32[1,1,1,8,128]{4,3,2,1,0:T(8,128)S(1)}, u32[]{:S(2)}, u32[]{:S(2)}) collective-permute-start(f32[1,1,1,8,128]{4,3,2,1,0:T(8,128)S(1)} %get-tuple-element.95), channel_id=1, source_target_pairs={{16,0},{0,16},{17,1},{1,17},{18,2},{2,18},{19,3},{3,19},{20,4},{4,... | collective-permute-start | bytes 12296 | tf_op jit(solution)/shard_map/ppermute | solution.py:13
  110.5 8.1 %collective-permute-start.13 = (f32[1,1,1,8,128]{4,3,2,1,0:T(8,128)S(1)}, f32[1,1,1,8,128]{4,3,2,1,0:T(8,128)S(1)}, u32[]{:S(2)}, u32[]{:S(2)}) collective-permute-start(f32[1,1,1,8,128]{4,3,2,1,0:T(8,128)S(1)} %get-tuple-element.94), channel_id=1, source_target_pairs={{16,0},{0,16},{17,1},{1,17},{18,2},{2,18},{19,3},{3,19},{20,4},{4,... | collective-permute-start | bytes 12296 | tf_op jit(solution)/shard_map/ppermute | solution.py:13
  110.9 7.7 collective-permute-start.14
  130.3 7.4 collective-permute-start.19
  130.8 6.9 collective-permute-start.20
  133.7 5.4 collective-permute-start.22
  181.3 6.0 collective-permute-start.24
  181.4 8.0 %collective-permute-start.25 = (f32[1,1,1,8,128]{4,3,2,1,0:T(8,128)S(1)}, f32[1,1,1,8,128]{4,3,2,1,0:T(8,128)S(1)}, u32[]{:S(2)}, u32[]{:S(2)}) collective-permute-start(f32[1,1,1,8,128]{4,3,2,1,0:T(8,128)S(1)} %get-tuple-element.88), channel_id=1, source_target_pairs={{16,0},{0,16},{17,1},{1,17},{18,2},{2,18},{19,3},{3,19},{20,4},{4,... | collective-permute-start | bytes 12296 | tf_op jit(solution)/shard_map/ppermute | solution.py:13
  181.9 7.5 collective-permute-start.26
  259.1 5.5 collective-permute-start.30
  261.6 6.8 collective-permute-start.31
  261.7 6.8 collective-permute-start.32
  262.7 9.4 %collective-permute-start.33 = (f32[1,1,1,8,128]{4,3,2,1,0:T(8,128)S(1)}, f32[1,1,1,8,128]{4,3,2,1,0:T(8,128)S(1)}, u32[]{:S(2)}, u32[]{:S(2)}) collective-permute-start(f32[1,1,1,8,128]{4,3,2,1,0:T(8,128)S(1)} %get-tuple-element.38), channel_id=1, source_target_pairs={{4,0},{8,4},{12,8},{0,12},{5,1},{9,5},{13,9},{1,13},{6,2},{10,6},{... | collective-permute-start | bytes 12296 | tf_op jit(solution)/shard_map/ppermute | solution.py:13
  264.6 7.5 collective-permute-start.34
  264.6 7.5 collective-permute-start.35
  314.7 6.4 collective-permute-start.36
  314.7 8.1 %collective-permute-start.37 = (f32[1,1,1,8,128]{4,3,2,1,0:T(8,128)S(1)}, f32[1,1,1,8,128]{4,3,2,1,0:T(8,128)S(1)}, u32[]{:S(2)}, u32[]{:S(2)}) collective-permute-start(f32[1,1,1,8,128]{4,3,2,1,0:T(8,128)S(1)} %get-tuple-element.82), channel_id=1, source_target_pairs={{16,0},{0,16},{17,1},{1,17},{18,2},{2,18},{19,3},{3,19},{20,4},{4,... | collective-permute-start | bytes 12296 | tf_op jit(solution)/shard_map/ppermute | solution.py:13
  315.2 7.6 collective-permute-start.38
  334.9 7.3 collective-permute-start.43
  335.4 6.8 collective-permute-start.44
  336.1 6.1 collective-permute-start.45
  338.3 5.4 collective-permute-start.46
  383.2 6.0 collective-permute-start.48
  383.2 7.5 collective-permute-start.49
  383.7 7.1 collective-permute-start.50
  460.4 5.5 collective-permute-start.54
  463.0 6.8 collective-permute-start.55
  463.0 6.8 collective-permute-start.56
  464.5 9.4 %collective-permute-start.57 = (f32[1,1,1,8,128]{4,3,2,1,0:T(8,128)S(1)}, f32[1,1,1,8,128]{4,3,2,1,0:T(8,128)S(1)}, u32[]{:S(2)}, u32[]{:S(2)}) collective-permute-start(f32[1,1,1,8,128]{4,3,2,1,0:T(8,128)S(1)} %get-tuple-element.26), channel_id=1, source_target_pairs={{4,0},{8,4},{12,8},{0,12},{5,1},{9,5},{13,9},{1,13},{6,2},{10,6},{... | collective-permute-start | bytes 12296 | tf_op jit(solution)/shard_map/ppermute | solution.py:13
  466.0 8.0 %collective-permute-start.58 = (f32[1,1,1,8,128]{4,3,2,1,0:T(8,128)S(1)}, f32[1,1,1,8,128]{4,3,2,1,0:T(8,128)S(1)}, u32[]{:S(2)}, u32[]{:S(2)}) collective-permute-start(f32[1,1,1,8,128]{4,3,2,1,0:T(8,128)S(1)} %get-tuple-element.25), channel_id=1, source_target_pairs={{3,0},{0,1},{1,2},{2,3},{7,4},{4,5},{5,6},{6,7},{11,8},{8,9},{9,10... | collective-permute-start | bytes 12296 | tf_op jit(solution)/shard_map/ppermute | solution.py:13
  466.0 8.0 %collective-permute-start.59 = (f32[1,1,1,8,128]{4,3,2,1,0:T(8,128)S(1)}, f32[1,1,1,8,128]{4,3,2,1,0:T(8,128)S(1)}, u32[]{:S(2)}, u32[]{:S(2)}) collective-permute-start(f32[1,1,1,8,128]{4,3,2,1,0:T(8,128)S(1)} %get-tuple-element.24), channel_id=1, source_target_pairs={{1,0},{2,1},{3,2},{0,3},{5,4},{6,5},{7,6},{4,7},{9,8},{10,9},{11,1... | collective-permute-start | bytes 12296 | tf_op jit(solution)/shard_map/ppermute | solution.py:13
  516.6 6.4 collective-permute-start.60
  516.6 8.1 %collective-permute-start.61 = (f32[1,1,1,8,128]{4,3,2,1,0:T(8,128)S(1)}, f32[1,1,1,8,128]{4,3,2,1,0:T(8,128)S(1)}, u32[]{:S(2)}, u32[]{:S(2)}) collective-permute-start(f32[1,1,1,8,128]{4,3,2,1,0:T(8,128)S(1)} %get-tuple-element.70), channel_id=1, source_target_pairs={{16,0},{0,16},{17,1},{1,17},{18,2},{2,18},{19,3},{3,19},{20,4},{4,... | collective-permute-start | bytes 12296 | tf_op jit(solution)/shard_map/ppermute | solution.py:13
  517.1 7.6 collective-permute-start.62
  536.8 7.3 collective-permute-start.67
  537.3 6.8 collective-permute-start.68
  537.9 6.1 collective-permute-start.69
  540.2 5.4 collective-permute-start.70
  585.1 6.0 collective-permute-start.72
  585.1 7.5 collective-permute-start.73
  585.6 7.1 collective-permute-start.74
  662.3 5.5 collective-permute-start.78
  664.9 6.8 collective-permute-start.79
  664.9 6.8 collective-permute-start.80
  666.4 9.4 %collective-permute-start.81 = (f32[1,1,1,8,128]{4,3,2,1,0:T(8,128)S(1)}, f32[1,1,1,8,128]{4,3,2,1,0:T(8,128)S(1)}, u32[]{:S(2)}, u32[]{:S(2)}) collective-permute-start(f32[1,1,1,8,128]{4,3,2,1,0:T(8,128)S(1)} %get-tuple-element.14), channel_id=1, source_target_pairs={{4,0},{8,4},{12,8},{0,12},{5,1},{9,5},{13,9},{1,13},{6,2},{10,6},{... | collective-permute-start | bytes 12296 | tf_op jit(solution)/shard_map/ppermute | solution.py:13
  667.9 8.0 %collective-permute-start.82 = (f32[1,1,1,8,128]{4,3,2,1,0:T(8,128)S(1)}, f32[1,1,1,8,128]{4,3,2,1,0:T(8,128)S(1)}, u32[]{:S(2)}, u32[]{:S(2)}) collective-permute-start(f32[1,1,1,8,128]{4,3,2,1,0:T(8,128)S(1)} %get-tuple-element.13), channel_id=1, source_target_pairs={{3,0},{0,1},{1,2},{2,3},{7,4},{4,5},{5,6},{6,7},{11,8},{8,9},{9,10... | collective-permute-start | bytes 12296 | tf_op jit(solution)/shard_map/ppermute | solution.py:13
  667.9 8.0 %collective-permute-start.83 = (f32[1,1,1,8,128]{4,3,2,1,0:T(8,128)S(1)}, f32[1,1,1,8,128]{4,3,2,1,0:T(8,128)S(1)}, u32[]{:S(2)}, u32[]{:S(2)}) collective-permute-start(f32[1,1,1,8,128]{4,3,2,1,0:T(8,128)S(1)} %get-tuple-element.12), channel_id=1, source_target_pairs={{1,0},{2,1},{3,2},{0,3},{5,4},{6,5},{7,6},{4,7},{9,8},{10,9},{11,1... | collective-permute-start | bytes 12296 | tf_op jit(solution)/shard_map/ppermute | solution.py:13
  718.4 6.4 collective-permute-start.84
  718.5 8.1 %collective-permute-start.85 = (f32[1,1,1,8,128]{4,3,2,1,0:T(8,128)S(1)}, f32[1,1,1,8,128]{4,3,2,1,0:T(8,128)S(1)}, u32[]{:S(2)}, u32[]{:S(2)}) collective-permute-start(f32[1,1,1,8,128]{4,3,2,1,0:T(8,128)S(1)} %get-tuple-element.58), channel_id=1, source_target_pairs={{16,0},{0,16},{17,1},{1,17},{18,2},{2,18},{19,3},{3,19},{20,4},{4,... | collective-permute-start | bytes 12296 | tf_op jit(solution)/shard_map/ppermute | solution.py:13
  719.0 7.6 collective-permute-start.86
  738.7 7.3 collective-permute-start.91
  739.2 6.8 collective-permute-start.92
  739.9 6.1 collective-permute-start.93
  (36 other events, 556.3 us)
where the time goes:
time: 789 us; the launch traced here: 788 us
  blocking collectives  555 us (70%)
  starting transfers between devices  131 us (17%)
  matrix products  43.7 us (6%)
  waiting for transfers between devices  36.2 us (5%)
  local copies, waits for them, and re-layouts  12.5 us (2%)
    all_gather x4, blocking collectives, coarse_weights(): lax.all_gather(on_modes, ('gx', 'gy', 'gz'), axis=0, tiled=True)  268 us
    psum x4, blocking collectives, energy_sum(): lax.psum(partial_inner(first, second), ('gx', 'gy', 'gz')).reshape(-1, 1, 1)  169 us
    ppermute x96, starting transfers between devices, from_behind(): return lax.ppermute(block, axis, route)  131 us
    psum x3, blocking collectives, on_device(): lax.psum(partial_inner(direction, dual_image), ('gx', 'gy', 'gz'))  118 us
    dot_general x4, matrix products, on_device(): jnp.dot(local_flattened, matrix, precision=highest)  40.3 us
    ppermute x96, waiting for transfers between devices, from_behind(): return lax.ppermute(block, axis, route)  36.2 us
  transfers between devices with their start and end apart: 96, of which 24 were waited for; matrix products, arithmetic and copies ran while one was open for 1% of the time, Pallas kernels for 0%

commit v1 on v0

--- a/solution.py
+++ b/solution.py
@@ -110,7 +110,9 @@
     residual = start_vector
 
     def energy_sum(first, second):
-        return lax.psum(partial_inner(first, second), ("gx", "gy", "gz")).reshape(-1, 1, 1)
+        return lax.psum(lax.psum(partial_inner(first, second), ("gy", "gz")), "gx").reshape(
+            -1, 1, 1
+        )
 
     precond = project(residual)
     direction = precond

time: 789 us -> 838 us (1.062)
  blocking collectives: 555 us -> 607 us
    psum x3 -> x4, blocking collectives: 118 us -> 155 us  [on_device(): lax.psum(partial_inner(direction, dual_image), ('gx', 'gy', 'gz'))]
    psum x4 -> x8, blocking collectives: 169 us -> 184 us  [the longest x4 174 us: energy_sum(): lax.psum(partial_inner(first, second), ('gy', 'gz'))]
  transfers between devices with their start and end apart: 96 -> 96, of which waited for: 24 -> 20; matrix products, arithmetic and copies ran while one was open for 1% -> 1% of each run, Pallas kernels for 0% -> 0%
where the time goes in v1:
time: 838 us; the launch traced here: 837 us
  blocking collectives  607 us (72%)
  starting transfers between devices  128 us (15%)
  matrix products  43.7 us (5%)
  waiting for transfers between devices  35.9 us (4%)
  local copies, waits for them, and re-layouts  12.5 us (1%)
    all_gather x4, blocking collectives, coarse_weights(): lax.all_gather(on_modes, ('gx', 'gy', 'gz'), axis=0, tiled=True)  268 us
    psum x4, blocking collectives, energy_sum(): lax.psum(partial_inner(first, second), ('gy', 'gz'))  174 us
    psum x4, blocking collectives, on_device(): lax.psum(partial_inner(direction, dual_image), ('gx', 'gy', 'gz'))  155 us
    ppermute x96, starting transfers between devices, from_behind(): return lax.ppermute(block, axis, route)  128 us
    dot_general x4, matrix products, on_device(): jnp.dot(local_flattened, matrix, precision=highest)  40.3 us
    ppermute x96, waiting for transfers between devices, from_behind(): return lax.ppermute(block, axis, route)  35.9 us
  transfers between devices with their start and end apart: 96, of which 20 were waited for; matrix products, arithmetic and copies ran while one was open for 1% of the time, Pallas kernels for 0%

profile of v1, /device:TPU:0, one launch (start us, length us, event | category | flops | bytes accessed | tf_op | source)
XLA Modules:
  0.0 836.5 jit_solution(18280855844547458978)
XLA Ops:
  7.4 2.9 collective-permute-start.2
  11.2 2.1 collective-permute-start.4
  14.1 2.1 collective-permute-start.5
  18.8 67.1 %all-gather = f32[32,6,8]{2,1,0:T(8,128)S(1)} all-gather(f32[1,6,8]{2,1,0:T(8,128)S(1)} %bitcast.1086), channel_id=1, replica_groups=mesh['gx'=2,'gy'=4,'gz'=4] {'gx','gy','gz'}, dimensions={0}, use_global_device_ids=true | all-gather | bytes 6336 | tf_op jit(solution)/shard_map/all_gather | solution.py:57
  86.4 2.4 collective-permute-start.6
  88.9 1.6 collective-permute-start.8
  91.9 3.9 collective-permute-start.11
  95.7 4.1 collective-permute-done.9
  100.8 9.7 %copy.36 = f32[1,1,1,1536,1536]{3,4,2,1,0:T(8,128)} copy(f32[1,1,1,1536,1536]{4,3,2,1,0:T(8,128)} %param.6) | data formatting | bytes 18874368 | tf_op args[0]
  110.9 3.8 collective-permute-start.14
  114.7 3.9 collective-permute-start.17
  120.1 10.1 %convolution_bitcast_fusion.6 = f32[1,1,1,8,6,256]{5,3,4,2,1,0:T(8,128)S(1)} fusion(f32[8,1536,1]{1,0,2:T(8,128)S(1)} %bitcast.1078, f32[6,256,1536]{2,1,0:T(8,128)} %bitcast.1070), kind=kOutput, calls=%fused_computation.6 | convolution fusion | flops 226492416 | bytes 9535488 | tf_op jit(solution)/shard_map/dot_general | solution.py:125
  130.8 2.9 collective-permute-start.20
  134.8 2.8 collective-permute-start.23
  139.3 42.9 %psum.84 = f32[8]{0:T(128)S(1)} all-reduce(f32[8]{0:T(128)S(1)} %get-tuple-element.3), channel_id=1, replica_groups=mesh['gx'=2,'gy'=4,'gz'=4] {'gy','gz'}, use_global_device_ids=true, to_apply=%region_1.2 | all-reduce | flops 8 | bytes 64 | tf_op jit(solution)/shard_map/psum | solution.py:113
  182.2 2.5 psum.85
  184.6 36.8 %psum.86 = f32[8]{0:T(128)S(1)} all-reduce(f32[8]{0:T(128)S(1)} %get-tuple-element.2), channel_id=1, replica_groups=mesh['gx'=2,'gy'=4,'gz'=4] {'gx','gy','gz'}, use_global_device_ids=true, to_apply=%region_4.5 | all-reduce | flops 8 | bytes 64 | tf_op jit(solution)/shard_map/psum | solution.py:129
  222.1 2.3 collective-permute-start.26
  225.3 2.9 collective-permute-start.28
  229.2 1.5 collective-permute-done.28
  232.0 66.3 %all-gather.1 = f32[32,6,8]{2,1,0:T(8,128)S(1)} all-gather(f32[1,6,8]{2,1,0:T(8,128)S(1)} %bitcast.1087), channel_id=1, replica_groups=mesh['gx'=2,'gy'=4,'gz'=4] {'gx','gy','gz'}, dimensions={0}, use_global_device_ids=true | all-gather | bytes 6336 | tf_op jit(solution)/shard_map/all_gather | solution.py:57
  298.8 2.5 collective-permute-start.30
  304.4 3.8 collective-permute-start.35
  308.2 4.0 collective-permute-done.33
  312.4 43.7 %psum.87 = f32[8]{0:T(128)S(1)} all-reduce(f32[8]{0:T(128)S(1)} %multiply_reduce_fusion.5), channel_id=1, replica_groups=mesh['gx'=2,'gy'=4,'gz'=4] {'gy','gz'}, use_global_device_ids=true, to_apply=%region_6.7 | all-reduce | flops 8 | bytes 64 | tf_op jit(solution)/shard_map/psum | solution.py:113
  356.1 2.5 psum.88
  359.2 2.9 collective-permute-start.39
  362.2 3.8 collective-permute-start.41
  367.6 10.1 %convolution_bitcast_fusion.4 = f32[1,1,1,8,6,256]{5,3,4,2,1,0:T(8,128)S(1)} fusion(f32[8,1536,1]{1,0,2:T(8,128)S(1)} %bitcast.1079, f32[6,256,1536]{2,1,0:T(8,128)} %bitcast.1071), kind=kOutput, calls=%fused_computation.4 | convolution fusion | flops 226492416 | bytes 9535488 | tf_op jit(solution)/shard_map/dot_general | solution.py:125
  378.3 2.9 collective-permute-start.45
  381.2 3.8 collective-permute-start.47
  385.1 1.5 collective-permute-done.46
  386.7 39.5 %psum.89 = f32[8]{0:T(128)S(1)} all-reduce(f32[8]{0:T(128)S(1)} %multiply_reduce_fusion.4), channel_id=1, replica_groups=mesh['gx'=2,'gy'=4,'gz'=4] {'gx','gy','gz'}, use_global_device_ids=true, to_apply=%region_9.10 | all-reduce | flops 8 | bytes 64 | tf_op jit(solution)/shard_map/psum | solution.py:129
  426.8 2.3 collective-permute-start.50
  430.0 1.8 collective-permute-start.52
  431.8 2.0 collective-permute-start.53
  433.9 1.5 collective-permute-done.52
  435.7 67.3 %all-gather.2 = f32[32,6,8]{2,1,0:T(8,128)S(1)} all-gather(f32[1,6,8]{2,1,0:T(8,128)S(1)} %bitcast.1088), channel_id=1, replica_groups=mesh['gx'=2,'gy'=4,'gz'=4] {'gx','gy','gz'}, dimensions={0}, use_global_device_ids=true | all-gather | bytes 6336 | tf_op jit(solution)/shard_map/all_gather | solution.py:57
  503.5 2.5 collective-permute-start.54
  509.1 3.8 collective-permute-start.59
  512.9 4.1 collective-permute-done.57
  517.2 43.7 %psum.90 = f32[8]{0:T(128)S(1)} all-reduce(f32[8]{0:T(128)S(1)} %multiply_reduce_fusion.3), channel_id=1, replica_groups=mesh['gx'=2,'gy'=4,'gz'=4] {'gy','gz'}, use_global_device_ids=true, to_apply=%region_11.12 | all-reduce | flops 8 | bytes 64 | tf_op jit(solution)/shard_map/psum | solution.py:113
  560.9 2.5 psum.91
  564.0 2.9 collective-permute-start.63
  566.9 3.8 collective-permute-start.65
  572.3 10.1 %convolution_bitcast_fusion.2 = f32[1,1,1,8,6,256]{5,3,4,2,1,0:T(8,128)S(1)} fusion(f32[8,1536,1]{1,0,2:T(8,128)S(1)} %bitcast.1080, f32[6,256,1536]{2,1,0:T(8,128)} %bitcast.1072), kind=kOutput, calls=%fused_computation.2 | convolution fusion | flops 226492416 | bytes 9535488 | tf_op jit(solution)/shard_map/dot_general | solution.py:125
  583.0 2.9 collective-permute-start.69
  585.9 3.8 collective-permute-start.71
  591.5 39.5 %psum.92 = f32[8]{0:T(128)S(1)} all-reduce(f32[8]{0:T(128)S(1)} %multiply_reduce_fusion.2), channel_id=1, replica_groups=mesh['gx'=2,'gy'=4,'gz'=4] {'gx','gy','gz'}, use_global_device_ids=true, to_apply=%region_14.15 | all-reduce | flops 8 | bytes 64 | tf_op jit(solution)/shard_map/psum | solution.py:129
  631.6 2.3 collective-permute-start.74
  634.8 1.8 collective-permute-start.76
  636.6 2.0 collective-permute-start.77
  640.5 67.3 %all-gather.3 = f32[32,6,8]{2,1,0:T(8,128)S(1)} all-gather(f32[1,6,8]{2,1,0:T(8,128)S(1)} %bitcast.1089), channel_id=1, replica_groups=mesh['gx'=2,'gy'=4,'gz'=4] {'gx','gy','gz'}, dimensions={0}, use_global_device_ids=true | all-gather | bytes 6336 | tf_op jit(solution)/shard_map/all_gather | solution.py:57
  708.3 2.5 collective-permute-start.78
  713.8 3.8 collective-permute-start.83
  717.7 4.1 collective-permute-done.81
  721.9 43.7 %psum.93 = f32[8]{0:T(128)S(1)} all-reduce(f32[8]{0:T(128)S(1)} %multiply_reduce_fusion.1), channel_id=1, replica_groups=mesh['gx'=2,'gy'=4,'gz'=4] {'gy','gz'}, use_global_device_ids=true, to_apply=%region_16.17 | all-reduce | flops 8 | bytes 64 | tf_op jit(solution)/shard_map/psum | solution.py:113
  765.7 2.5 psum.94
  768.7 2.9 collective-permute-start.87
  771.7 3.8 collective-permute-start.89
  777.1 10.1 %convolution_bitcast_fusion = f32[1,1,1,8,6,256]{5,3,4,2,1,0:T(8,128)S(1)} fusion(f32[8,1536,1]{1,0,2:T(8,128)S(1)} %bitcast.1081, f32[6,256,1536]{2,1,0:T(8,128)} %bitcast.1073), kind=kOutput, calls=%fused_computation | convolution fusion | flops 226492416 | bytes 9535488 | tf_op jit(solution)/shard_map/dot_general | solution.py:125
  787.9 2.9 collective-permute-start.93
  790.8 3.8 collective-permute-start.95
  796.3 39.5 %psum.95 = f32[8]{0:T(128)S(1)} all-reduce(f32[8]{0:T(128)S(1)} %multiply_reduce_fusion), channel_id=1, replica_groups=mesh['gx'=2,'gy'=4,'gz'=4] {'gx','gy','gz'}, use_global_device_ids=true, to_apply=%region_19.20 | all-reduce | flops 8 | bytes 64 | tf_op jit(solution)/shard_map/psum | solution.py:129
  (321 shorter events, 51.8 us)
Async XLA Ops:
  6.8 7.2 collective-permute-start
  7.3 8.9 %collective-permute-start.1 = (f32[1,1,1,8,128]{4,3,2,1,0:T(8,128)S(1)}, f32[1,1,1,8,128]{4,3,2,1,0:T(8,128)S(1)}, u32[]{:S(2)}, u32[]{:S(2)}) collective-permute-start(f32[1,1,1,8,128]{4,3,2,1,0:T(8,128)S(1)} %get-tuple-element.98), channel_id=1, source_target_pairs={{16,0},{0,16},{17,1},{1,17},{18,2},{2,18},{19,3},{3,19},{20,4},{4,... | collective-permute-start | bytes 12296 | tf_op jit(solution)/shard_map/ppermute | solution.py:13
  7.4 8.8 %collective-permute-start.2 = (f32[1,1,1,8,128]{4,3,2,1,0:T(8,128)S(1)}, f32[1,1,1,8,128]{4,3,2,1,0:T(8,128)S(1)}, u32[]{:S(2)}, u32[]{:S(2)}) collective-permute-start(f32[1,1,1,8,128]{4,3,2,1,0:T(8,128)S(1)} %get-tuple-element.97), channel_id=1, source_target_pairs={{12,0},{0,4},{4,8},{8,12},{13,1},{1,5},{5,9},{9,13},{14,2},{2,6},{... | collective-permute-start | bytes 12296 | tf_op jit(solution)/shard_map/ppermute | solution.py:13
  10.3 5.9 collective-permute-start.3
  11.2 5.7 collective-permute-start.4
  86.4 5.4 collective-permute-start.6
  88.8 6.9 collective-permute-start.7
  88.9 6.8 collective-permute-start.8
  90.5 9.4 %collective-permute-start.9 = (f32[1,1,1,8,128]{4,3,2,1,0:T(8,128)S(1)}, f32[1,1,1,8,128]{4,3,2,1,0:T(8,128)S(1)}, u32[]{:S(2)}, u32[]{:S(2)}) collective-permute-start(f32[1,1,1,8,128]{4,3,2,1,0:T(8,128)S(1)} %get-tuple-element.48), channel_id=1, source_target_pairs={{4,0},{8,4},{12,8},{0,12},{5,1},{9,5},{13,9},{1,13},{6,2},{10,6},{... | collective-permute-start | bytes 12296 | tf_op jit(solution)/shard_map/ppermute | solution.py:13
  91.8 8.0 collective-permute-start.10
  91.9 8.0 collective-permute-start.11
  100.7 14.0 %collective-permute-start.12 = (f32[1,1,1,8,128]{4,3,2,1,0:T(8,128)S(1)}, f32[1,1,1,8,128]{4,3,2,1,0:T(8,128)S(1)}, u32[]{:S(2)}, u32[]{:S(2)}) collective-permute-start(f32[1,1,1,8,128]{4,3,2,1,0:T(8,128)S(1)} %get-tuple-element.93), channel_id=1, source_target_pairs={{16,0},{0,16},{17,1},{1,17},{18,2},{2,18},{19,3},{3,19},{20,4},{4,... | collective-permute-start | bytes 12296 | tf_op jit(solution)/shard_map/ppermute | solution.py:13
  110.4 8.1 collective-permute-start.13
  110.9 7.7 collective-permute-start.14
  114.7 5.4 collective-permute-start.16
  130.3 7.4 collective-permute-start.19
  130.8 6.9 collective-permute-start.20
  133.7 5.4 collective-permute-start.22
  221.5 6.6 collective-permute-start.24
  221.6 7.6 collective-permute-start.25
  222.1 7.1 collective-permute-start.26
  225.3 5.4 collective-permute-start.28
  298.8 5.5 collective-permute-start.30
  301.3 6.8 collective-permute-start.31
  301.4 6.8 collective-permute-start.32
  302.9 9.4 %collective-permute-start.33 = (f32[1,1,1,8,128]{4,3,2,1,0:T(8,128)S(1)}, f32[1,1,1,8,128]{4,3,2,1,0:T(8,128)S(1)}, u32[]{:S(2)}, u32[]{:S(2)}) collective-permute-start(f32[1,1,1,8,128]{4,3,2,1,0:T(8,128)S(1)} %get-tuple-element.36), channel_id=1, source_target_pairs={{4,0},{8,4},{12,8},{0,12},{5,1},{9,5},{13,9},{1,13},{6,2},{10,6},{... | collective-permute-start | bytes 12296 | tf_op jit(solution)/shard_map/ppermute | solution.py:13
  304.3 7.9 collective-permute-start.34
  304.4 7.9 collective-permute-start.35
  358.9 7.1 collective-permute-start.37
  359.2 6.8 collective-permute-start.38
  359.2 6.8 collective-permute-start.39
  377.8 7.3 collective-permute-start.43
  378.3 6.8 collective-permute-start.44
  378.3 6.8 collective-permute-start.45
  426.3 5.6 collective-permute-start.48
  426.3 7.5 collective-permute-start.49
  426.8 7.0 collective-permute-start.50
  503.5 5.5 collective-permute-start.54
  506.1 6.8 collective-permute-start.55
  506.1 6.8 collective-permute-start.56
  507.6 9.4 %collective-permute-start.57 = (f32[1,1,1,8,128]{4,3,2,1,0:T(8,128)S(1)}, f32[1,1,1,8,128]{4,3,2,1,0:T(8,128)S(1)}, u32[]{:S(2)}, u32[]{:S(2)}) collective-permute-start(f32[1,1,1,8,128]{4,3,2,1,0:T(8,128)S(1)} %get-tuple-element.24), channel_id=1, source_target_pairs={{4,0},{8,4},{12,8},{0,12},{5,1},{9,5},{13,9},{1,13},{6,2},{10,6},{... | collective-permute-start | bytes 12296 | tf_op jit(solution)/shard_map/ppermute | solution.py:13
  509.1 7.9 collective-permute-start.58
  509.1 8.0 collective-permute-start.59
  563.6 7.1 collective-permute-start.61
  564.0 6.8 collective-permute-start.62
  564.0 6.8 collective-permute-start.63
  582.5 7.3 collective-permute-start.67
  583.0 6.8 collective-permute-start.68
  583.0 6.8 collective-permute-start.69
  631.1 5.5 collective-permute-start.72
  631.1 7.5 collective-permute-start.73
  631.6 7.0 collective-permute-start.74
  708.3 5.5 collective-permute-start.78
  710.8 6.8 collective-permute-start.79
  710.9 6.8 collective-permute-start.80
  712.4 9.4 %collective-permute-start.81 = (f32[1,1,1,8,128]{4,3,2,1,0:T(8,128)S(1)}, f32[1,1,1,8,128]{4,3,2,1,0:T(8,128)S(1)}, u32[]{:S(2)}, u32[]{:S(2)}) collective-permute-start(f32[1,1,1,8,128]{4,3,2,1,0:T(8,128)S(1)} %get-tuple-element.12), channel_id=1, source_target_pairs={{4,0},{8,4},{12,8},{0,12},{5,1},{9,5},{13,9},{1,13},{6,2},{10,6},{... | collective-permute-start | bytes 12296 | tf_op jit(solution)/shard_map/ppermute | solution.py:13
  713.8 7.9 collective-permute-start.82
  713.8 7.9 collective-permute-start.83
  768.4 7.1 collective-permute-start.85
  768.7 6.8 collective-permute-start.86
  768.7 6.8 collective-permute-start.87
  787.3 7.3 collective-permute-start.91
  787.8 6.8 collective-permute-start.92
  787.9 6.8 collective-permute-start.93
  (36 other events, 599.4 us)
